TPU v7x, 32 devices: a whole 2x2x4 slice. The times are simulated.
32 devices in a mesh: rep: 2 (over y), col: 16 (over z, x, core).
Axes of the slice: x: 2, y: 2, z: 4, core: 2. Of those that a mesh axis runs over, the one named last changes fastest.
Arguments:
- alignment: bfloat16 [64, 32, 768], P('rep', 'col'), parts along dimension 0, may hold values from -4 to 4
- norm_gain: bfloat16 [768], replicated, may hold values from 0.099609375 to 1.8984375
- norm_bias: bfloat16 [768], replicated, may hold values from -3 to 3
- w_query: bfloat16 [768, 768], replicated, may hold values from -1 to 1
- w_key: bfloat16 [768, 768], replicated, may hold values from -1 to 1
- w_value: bfloat16 [768, 768], replicated, may hold values from -0.21875 to 0.21875
- w_out: bfloat16 [768, 768], replicated, may hold values from -0.21875 to 0.21875
Outputs:
- update: bfloat16 [64, 32, 768], P('rep', 'col'), parts along dimension 0
There are 2 independent parts, one for each index of `rep`. A program takes and returns all parts, laid end to end along the dimension named above; an argument that names none is the same for every part. Nothing has to cross between parts.
All inputs are finite; a program needn't handle non-finite values.
Results may differ from a plain program's by a relative error of at most 0.004.
The roundings to bfloat16 on the way count: a program that leaves them out, or rounds other values in their place, can miss the bound.
Values may be sent and summed in bfloat16 or wider, within the bound.
A program may use at most 64 MiB of HBM per device.

v0:
```python
import math

import jax
import jax.numpy as jnp
from jax import lax
from jax.sharding import PartitionSpec as P

HEADS = 12


def normalize(tokens, norm_gain, norm_bias):
    values_f = tokens.astype(jnp.float32)
    center = jnp.mean(values_f, axis=-1, keepdims=True)
    spread = jnp.mean((values_f - center) ** 2, axis=-1, keepdims=True)
    scaled = (values_f - center) * lax.rsqrt(spread + 1e-05)
    return (scaled * norm_gain.astype(jnp.float32) + norm_bias.astype(jnp.float32)).astype(
        jnp.bfloat16
    )


def project_heads(normed_flat, weight, factor, shape_out):
    product = jnp.dot(normed_flat, weight, preferred_element_type=jnp.float32) * factor
    return product.astype(jnp.bfloat16).reshape(shape_out)


def softmax_rows(logits):
    highest = jnp.max(logits, axis=-1, keepdims=True)
    expo = jnp.exp(logits - highest)
    return (expo / jnp.sum(expo, axis=-1, keepdims=True)).astype(jnp.bfloat16)


def local(alignment, norm_gain, norm_bias, w_query, w_key, w_value, w_out):
    local_rows = lax.all_to_all(alignment, "col", split_axis=0, concat_axis=1, tiled=True)
    seq_dev, columns, model_width = local_rows.shape
    head_size = model_width // HEADS
    total_seqs = seq_dev * lax.axis_size("col")
    head_shape = (seq_dev, columns, HEADS, head_size)
    normed_flat = normalize(local_rows, norm_gain, norm_bias).reshape(-1, model_width)
    queries = project_heads(
        normed_flat, w_query, 1.0 / math.sqrt(head_size * total_seqs), head_shape
    )
    key_rows = project_heads(normed_flat, w_key, 1.0, head_shape)
    value_rows = project_heads(normed_flat, w_value, 1.0, head_shape)
    partial_sum = jnp.einsum(
        "sihd,sjhd->ihj", queries, key_rows, preferred_element_type=jnp.float32
    )
    summed = lax.psum(partial_sum, "col")
    weights = softmax_rows(summed)
    mixed = jnp.einsum("ihj,sjhd->sihd", weights, value_rows, preferred_element_type=jnp.float32)
    mixed = mixed.astype(jnp.bfloat16).reshape(-1, model_width)
    result = jnp.dot(mixed, w_out, preferred_element_type=jnp.float32).astype(jnp.bfloat16)
    result = result.reshape(seq_dev, columns, model_width)
    return lax.all_to_all(result, "col", split_axis=1, concat_axis=0, tiled=True)


def solution(mesh):
    placed = (P("rep", "col", None), P(), P(), P(), P(), P(), P())
    return jax.shard_map(
        local, mesh=mesh, in_specs=placed, out_specs=P("rep", "col", None), check_vma=False
    )
```

profile of v0, /device:TPU:0, one launch (start us, length us, event | category | flops | bytes accessed | tf_op | source)
XLA Modules:
  0.0 90.2 jit_solution(13145598110946689584)
XLA Ops:
  0.0 0.0 copy-start
  0.0 7.5 %all-to-all-start = ((bf16[32,2,768]{2,1,0:T(2,128)(2,1)}), bf16[32,2,768]{2,1,0:T(2,128)(2,1)S(1)}, u32[]{:S(2)}, u32[]{:S(2)}) async-start(bf16[32,2,768]{2,1,0:T(2,128)(2,1)} %param.7), calls=%async_computation | async-start | bytes 196608 | tf_op jit(solution)/shard_map/all_to_all | solution.py:33
  7.5 0.7 convert_element_type.55
  8.2 0.7 convert_element_type.56
  8.9 6.0 %all-to-all-done = bf16[32,2,768]{2,1,0:T(2,128)(2,1)S(1)} async-done(((bf16[32,2,768]{2,1,0:T(2,128)(2,1)}), bf16[32,2,768]{2,1,0:T(2,128)(2,1)S(1)}, u32[]{:S(2)}, u32[]{:S(2)}) %all-to-all-start) | async-done | bytes 98336 | tf_op jit(solution)/shard_map/all_to_all | solution.py:33
  14.9 0.1 bitcast_convert_fusion
  15.0 0.1 fusion.10
  15.1 0.2 multiply_reduce_fusion
  15.4 0.1 div.17
  15.5 0.1 rsqrt.12
  15.6 0.1 copy_bitcast_fusion
  15.7 0.0 copy-start.1
  15.7 0.1 reshape.65
  15.8 0.0 copy-done
  15.8 0.4 convolution_convert_fusion.2
  16.2 0.2 reshape.61
  16.4 0.6 copy-done.1
  16.9 0.4 fusion.4
  17.3 0.0 copy-start.2
  17.3 0.2 reshape.62
  17.5 0.2 convolution_bitcast_fusion
  17.7 59.6 %psum.7 = f32[32,12,32]{0,2,1:T(8,128)S(1)} all-reduce(f32[32,12,32]{0,2,1:T(8,128)S(1)} %convolution_bitcast_fusion), channel_id=1, replica_groups=mesh['rep'=2,'col'=16] {'col'}, use_global_device_ids=true, to_apply=%region_2.0 | all-reduce | flops 12288 | bytes 98304 | tf_op jit(solution)/shard_map/psum | solution.py:47
  77.3 0.1 fusion.11
  77.4 0.0 copy-done.2
  77.4 0.4 convolution_convert_fusion.3
  77.8 0.0 copy-start.3
  77.8 0.2 reshape.60
  77.9 0.3 fusion.2
  78.2 0.1 copy.26
  78.4 0.2 reshape.63
  78.5 0.5 copy-done.3
  79.0 0.3 convolution_convert_fusion.1
  79.4 0.1 copy.27
  79.5 10.0 %all_to_all.27 = bf16[2,32,768]{2,0,1:T(2,128)(2,1)S(1)} all-to-all(bf16[2,32,768]{2,0,1:T(2,128)(2,1)S(1)} %copy.27), channel_id=1, replica_groups=mesh['rep'=2,'col'=16] {'col'}, dimensions={1} | all-to-all | bytes 196608 | tf_op jit(solution)/shard_map/all_to_all | solution.py:53
  89.5 0.7 copy.28
  (2 shorter events, 0.0 us)
Async XLA Ops:
  0.0 15.8 %copy-start = (bf16[768,768]{1,0:T(8,128)(2,1)S(1)}, bf16[768,768]{1,0:T(8,128)(2,1)}, u32[]{:S(2)}) copy-start(bf16[768,768]{1,0:T(8,128)(2,1)} %param.11) | copy-start | bytes 3538948
  0.0 14.9 %all-to-all-start = ((bf16[32,2,768]{2,1,0:T(2,128)(2,1)}), bf16[32,2,768]{2,1,0:T(2,128)(2,1)S(1)}, u32[]{:S(2)}, u32[]{:S(2)}) async-start(bf16[32,2,768]{2,1,0:T(2,128)(2,1)} %param.7), calls=%async_computation | async-start | bytes 196608 | tf_op jit(solution)/shard_map/all_to_all | solution.py:33
  15.7 1.3 %copy-start.1 = (bf16[768,768]{1,0:T(8,128)(2,1)S(1)}, bf16[768,768]{1,0:T(8,128)(2,1)}, u32[]{:S(2)}) copy-start(bf16[768,768]{1,0:T(8,128)(2,1)} %param.10) | copy-start | bytes 3538948
  17.3 60.1 %copy-start.2 = (bf16[768,768]{1,0:T(8,128)(2,1)S(1)}, bf16[768,768]{1,0:T(8,128)(2,1)}, u32[]{:S(2)}) copy-start(bf16[768,768]{1,0:T(8,128)(2,1)} %param.12) | copy-start | bytes 3538948
  77.8 1.3 %copy-start.3 = (bf16[768,768]{1,0:T(8,128)(2,1)S(1)}, bf16[768,768]{1,0:T(8,128)(2,1)}, u32[]{:S(2)}) copy-start(bf16[768,768]{1,0:T(8,128)(2,1)} %param.13) | copy-start | bytes 3538948
where the time goes:
time: 90.6 us; the launch traced here: 90.2 us
  blocking collectives  69.6 us (77%)
  starting transfers between devices  7.49 us (8%)
  waiting for transfers between devices  6.04 us (7%)
  local copies, waits for them, and re-layouts  3.04 us (3%)
  other arithmetic  1.95 us (2%)
  matrix products  1.89 us (2%)
    psum x1, blocking collectives, local(): summed = lax.psum(partial_sum, 'col')  59.6 us
    all_to_all x1, blocking collectives, local(): lax.all_to_all(result, 'col', split_axis=1, concat_axis=0, tiled=True)  9.99 us
    all_to_all x1, starting transfers between devices, local(): lax.all_to_all(alignment, 'col', split_axis=0, concat_axis=1, tiled=True)  7.49 us
    all_to_all x1, waiting for transfers between devices, local(): lax.all_to_all(alignment, 'col', split_axis=0, concat_axis=1, tiled=True)  6.04 us
  transfers between devices with their start and end apart: 1, of which 1 were waited for; matrix products, arithmetic and copies ran while one was open for 2% of the time, Pallas kernels for 0%

commit v1 on v0

v1 whole, which is shorter than its diff:
```python
import functools
import math

import jax
import jax.numpy as jnp
from jax import lax
from jax.experimental import pallas as pl
from jax.experimental.pallas import tpu as pltpu
from jax.sharding import PartitionSpec as P

HEADS = 12
MESH = pl.DeviceIdType.MESH


def each(count, body):
    if count <= 16:
        for k in range(count):
            body(k)
    else:
        lax.fori_loop(0, count, lambda k, c: (body(k), c)[1], 0)


def scatter_rows(n, cd, source, put):
    if n <= 16:
        for p in range(n):
            put(p, source[p * cd : (p + 1) * cd, :])
        return
    per = max(8 // cd, 1)

    def body(q):
        tile = source[pl.ds(pl.multiple_of(q * per * cd, per * cd), per * cd), :]
        for k in range(per):
            put(q * per + k, tile[k * cd : (k + 1) * cd, :])

    each(n // per, body)


def gather_rows(n, cd, take, target):
    if n <= 16:
        for p in range(n):
            target[p * cd : (p + 1) * cd, :] = take(p)
        return
    per = max(8 // cd, 1)

    def body(q):
        tile = jnp.concatenate([take(q * per + k) for k in range(per)], axis=0)
        target[pl.ds(pl.multiple_of(q * per * cd, per * cd), per * cd), :] = tile

    each(n // per, body)


def drain(like, sem):
    pltpu.make_async_copy(like, like, sem).wait()


def kernel(
    n, x, gain, bias, wq, wk, wv, wo, out,
    toks, rows, gb, bb, ws, lg, lg_send, lg_recv, wt_all, wt, back, fill, load_sem, own_sem, send_sem, recv_sem,
):
    me = lax.axis_index("col")
    sd, cd, width = toks.shape[1:]
    cols = n * cd
    head = width // HEADS
    total = sd * cols

    barrier = pltpu.get_barrier_semaphore()

    def peer(k):
        return lax.rem(me + k, n)

    def greet(k):
        pl.semaphore_signal(barrier, inc=1, device_id={"col": peer(k + 1)}, device_id_type=MESH)

    each(n - 1, greet)
    loads = []
    for k, w in enumerate((wq, wk, wv, wo)):
        loads.append(pltpu.make_async_copy(w, ws.at[k], load_sem.at[k]))
    loads.append(pltpu.make_async_copy(gain, gb, load_sem.at[4]))
    loads.append(pltpu.make_async_copy(bias, bb, load_sem.at[5]))
    own_in = pltpu.make_async_copy(x.at[pl.ds(me * sd, sd)], toks.at[me], own_sem.at[0])
    pl.semaphore_wait(barrier, n - 1)

    def remote(src, dst, phase, p):
        pltpu.make_async_remote_copy(
            src_ref=src, dst_ref=dst, send_sem=send_sem.at[phase], recv_sem=recv_sem.at[phase],
            device_id={"col": p}, device_id_type=MESH,
        ).start()

    def send_tokens(k):
        p = peer(k + 1)
        remote(x.at[pl.ds(p * sd, sd)], toks.at[me], 0, p)

    each(n - 1, send_tokens)
    own_in.start()
    for k in (4, 5, 0, 1, 2, 3):
        loads[k].start()
    loads[4].wait()
    loads[5].wait()
    gain_f = gb[...].astype(jnp.float32).reshape(1, width)
    bias_f = bb[...].astype(jnp.float32).reshape(1, width)
    own_in.wait()
    others = pl.ds(0, n - 1)
    drain(toks.at[others], recv_sem.at[0])

    for s in range(sd):
        gather_rows(
            n, cd, lambda p: toks[p, s].astype(jnp.float32), rows.at[pl.ds(s * cols, cols)]
        )
    a = rows[...]
    center = jnp.sum(a, axis=-1, keepdims=True) * (1.0 / width)
    shifted = a - center
    spread = jnp.sum(shifted * shifted, axis=-1, keepdims=True) * (1.0 / width)
    normed = (shifted * lax.rsqrt(spread + 1e-05) * gain_f + bias_f).astype(jnp.bfloat16)

    def project(k, factor):
        product = jnp.dot(normed, ws[k], preferred_element_type=jnp.float32)
        return (product * factor if factor != 1.0 else product).astype(jnp.bfloat16)

    group = 4
    wide = group * head
    lane = lax.broadcasted_iota(jnp.int32, (cols, wide), 1)

    def spread_heads(block):
        zero = jnp.zeros_like(block)
        return jnp.concatenate(
            [
                jnp.where((lane >= h * head) & (lane < (h + 1) * head), block, zero)
                for h in range(group)
            ],
            axis=0,
        )

    loads[0].wait()
    queries = project(0, 1.0 / math.sqrt(head * sd * n))
    loads[1].wait()
    keys = project(1, 1.0)
    for g in range(HEADS // group):
        f = slice(g * wide, (g + 1) * wide)
        acc = None
        for s in range(sd):
            r = slice(s * cols, (s + 1) * cols)
            part = lax.dot_general(
                queries[r, f], spread_heads(keys[r, f]), (((1,), (1,)), ((), ())),
                preferred_element_type=jnp.float32,
            )
            acc = part if acc is None else acc + part
        lg[:, g * group * cols : (g + 1) * group * cols] = acc

    def pack_logits(p, block):
        lg_send[p] = block

    scatter_rows(n, cd, lg, pack_logits)
    lg_recv[me] = lg_send[me]

    def send_logits(k):
        p = peer(k + 1)
        remote(lg_send.at[p], lg_recv.at[me], 1, p)

    each(n - 1, send_logits)

    loads[2].wait()
    vals = project(2, 1.0)

    drain(lg_recv.at[others], recv_sem.at[1])
    span = max(cols, 128)
    per = span // cols
    seg = lax.broadcasted_iota(jnp.int32, (cd, span), 1)
    for c in range(HEADS // per):
        part = slice(c * span, (c + 1) * span)
        if n <= 16:
            logits = lg_recv[0, :, part]
            for p in range(1, n):
                logits = logits + lg_recv[p, :, part]
        else:
            logits = lax.fori_loop(
                1, n, lambda p, t: t + lg_recv[p, :, part], lg_recv[0, :, part]
            )
        inside = [(seg >= k * cols) & (seg < (k + 1) * cols) for k in range(per)]
        highest = jnp.zeros_like(logits)
        for m in inside:
            top = jnp.max(jnp.where(m, logits, -jnp.inf), axis=-1, keepdims=True)
            highest = jnp.where(m, top, highest)
        expo = jnp.exp(logits - highest)
        norm = jnp.zeros_like(logits)
        for m in inside:
            norm = jnp.where(m, jnp.sum(jnp.where(m, expo, 0.0), axis=-1, keepdims=True), norm)
        wt_all[me, :, part] = (expo / norm).astype(jnp.bfloat16)

    def send_weights(k):
        remote(wt_all.at[me], wt_all.at[me], 2, peer(k + 1))

    each(n - 1, send_weights)
    loads[3].wait()
    drain(wt_all.at[others], recv_sem.at[2])

    gather_rows(n, cd, lambda p: wt_all[p].astype(jnp.float32), wt)
    weights = wt[...].astype(jnp.bfloat16)
    blocks = []
    for s in range(sd):
        r = slice(s * cols, (s + 1) * cols)
        line = []
        for g in range(HEADS // group):
            line.append(
                jnp.dot(
                    weights[:, g * group * cols : (g + 1) * group * cols],
                    spread_heads(vals[r, g * wide : (g + 1) * wide]),
                    preferred_element_type=jnp.float32,
                ).astype(jnp.bfloat16)
            )
        blocks.append(jnp.concatenate(line, axis=1))
    mixed = jnp.concatenate(blocks, axis=0)
    fill[...] = jnp.dot(mixed, ws[3], preferred_element_type=jnp.float32)

    for s in range(sd):

        def pack_back(p, block):
            back[p, s] = block.astype(jnp.bfloat16)

        scatter_rows(n, cd, fill.at[pl.ds(s * cols, cols)], pack_back)

    def send_back(k):
        p = peer(k + 1)
        remote(back.at[p], out.at[pl.ds(me * sd, sd)], 3, p)

    each(n - 1, send_back)
    own_out = pltpu.make_async_copy(back.at[me], out.at[pl.ds(me * sd, sd)], own_sem.at[1])
    own_out.start()
    drain(toks.at[others], send_sem.at[0])
    drain(lg_send.at[others], send_sem.at[1])
    drain(wt_all.at[others], send_sem.at[2])
    drain(back.at[others], send_sem.at[3])
    own_out.wait()
    drain(out.at[pl.ds(0, sd * (n - 1))], recv_sem.at[3])


def local(n, x, *params):
    seqs, cd, width = x.shape
    sd = seqs // n
    cols = n * cd
    bf, f32 = jnp.bfloat16, jnp.float32
    tokens = sd * cols
    anywhere = pl.BlockSpec(memory_space=pl.ANY)
    return pl.pallas_call(
        functools.partial(kernel, n),
        out_shape=jax.ShapeDtypeStruct(x.shape, bf),
        in_specs=[anywhere] * 7,
        out_specs=anywhere,
        scratch_shapes=[
            pltpu.VMEM((n, sd, cd, width), bf),
            pltpu.VMEM((tokens, width), f32),
            pltpu.VMEM((width,), bf),
            pltpu.VMEM((width,), bf),
            pltpu.VMEM((4, width, width), bf),
            pltpu.VMEM((cols, HEADS * cols), f32),
            pltpu.VMEM((n, cd, HEADS * cols), f32),
            pltpu.VMEM((n, cd, HEADS * cols), f32),
            pltpu.VMEM((n, cd, HEADS * cols), bf),
            pltpu.VMEM((cols, HEADS * cols), f32),
            pltpu.VMEM((n, sd, cd, width), bf),
            pltpu.VMEM((tokens, width), f32),
            pltpu.SemaphoreType.DMA((6,)),
            pltpu.SemaphoreType.DMA((2,)),
            pltpu.SemaphoreType.DMA((4,)),
            pltpu.SemaphoreType.DMA((4,)),
        ],
        compiler_params=pltpu.CompilerParams(
            collective_id=0, has_side_effects=True, vmem_limit_bytes=56 * 2**20
        ),
    )(x, *params)


def solution(mesh):
    placed = (P("rep", "col", None), P(), P(), P(), P(), P(), P())
    return jax.shard_map(
        functools.partial(local, mesh.shape["col"]),
        mesh=mesh, in_specs=placed, out_specs=P("rep", "col", None), check_vma=False,
    )
```

time: 90.6 us -> 27 us (0.30)
  blocking collectives: 69.6 us -> 0 us
  Pallas kernels: 0 us -> 25.2 us
  starting transfers between devices: 7.49 us -> 0 us
  waiting for transfers between devices: 6.04 us -> 0 us
  other arithmetic: 1.95 us -> 0 us
  matrix products: 1.89 us -> 0 us
  local copies, waits for them, and re-layouts: 3.04 us -> 1.6 us
    psum x1 -> x0, blocking collectives: 59.6 us -> none  [local(): summed = lax.psum(partial_sum, 'col')]
    pallas_call x0 -> x1, Pallas kernels: none -> 25.2 us  [local(): pl.pallas_call(functools.partial(kernel, n), out_shape=jax.ShapeDtypeStru...]
    all_to_all x1 -> x0, blocking collectives: 9.99 us -> none  [local(): lax.all_to_all(result, 'col', split_axis=1, concat_axis=0, tiled=True)]
    all_to_all x1 -> x0, starting transfers between devices: 7.49 us -> none  [local(): lax.all_to_all(alignment, 'col', split_axis=0, concat_axis=1, tiled=True)]
    all_to_all x1 -> x0, waiting for transfers between devices: 6.04 us -> none  [local(): lax.all_to_all(alignment, 'col', split_axis=0, concat_axis=1, tiled=True)]
    dot_general x6 -> x0, matrix products: 1.89 us -> none  [the longest x3 1.11 us: project_heads(): jnp.dot(normed_flat, weight, preferred_element_type=jnp.float32) * factor]
    convert_element_type x4 -> x0, other arithmetic: 1.51 us -> none  [the longest x1 0.69 us: normalize(): norm_gain.astype(jnp.float32)]
  transfers between devices with their start and end apart: 1 -> 0, of which waited for: 1 -> 0; matrix products, arithmetic and copies ran while one was open for 2% -> 0% of each run, Pallas kernels for 0% -> 0%
where the time goes in v1:
time: 27 us; the launch traced here: 26.8 us
  Pallas kernels  25.2 us (93%)
  local copies, waits for them, and re-layouts  1.6 us (6%)
    pallas_call x1, Pallas kernels, local(): pl.pallas_call(functools.partial(kernel, n), out_shape=jax.ShapeDtypeStru...  25.2 us
    unnamed x1, local copies, waits for them, and re-layouts  1.6 us

profile of v1, /device:TPU:0, one launch (start us, length us, event | category | flops | bytes accessed | tf_op | source)
XLA Modules:
  0.0 26.8 jit_solution(5858003267379693617)
XLA Ops:
  0.0 25.2 %shard_map.73 = bf16[32,2,768]{2,1,0:T(2,128)(2,1)} custom-call(bf16[32,2,768]{2,1,0:T(2,128)(2,1)} %x.1, bf16[768]{0:T(1024)(128)(2,1)} %gain.1, bf16[768]{0:T(1024)(128)(2,1)} %bias.1, bf16[768,768]{1,0:T(8,128)(2,1)} %wq.1, bf16[768,768]{1,0:T(8,128)(2,1)} %wk.1, bf16[768,768]{1,0:T(8,128)(2,1)} %wv.1, bf16[768,768]{1,0:T(8,128)(2,1)} %wo.1), custom_call_target="tpu_custom_call" | custom-call | tf_op jit(solution)/shard_map/pallas_call | solution.py:243
  25.2 1.6 %copy.9 = bf16[32,2,768]{2,1,0:T(2,128)(2,1)} copy(bf16[32,2,768]{2,1,0:T(2,128)(2,1)} %shard_map.73) | data formatting | bytes 196608

commit v2 on v1

--- a/solution.py
+++ b/solution.py
@@ -20,6 +20,16 @@
         lax.fori_loop(0, count, lambda k, c: (body(k), c)[1], 0)
 
 
+def around(n, body):
+    def pair(k):
+        body(k + 1)
+        body(n - 1 - k)
+
+    each((n - 1) // 2, pair)
+    if n % 2 == 0:
+        body(n // 2)
+
+
 def scatter_rows(n, cd, source, put):
     if n <= 16:
         for p in range(n):
@@ -55,7 +65,7 @@
 
 def kernel(
     n, x, gain, bias, wq, wk, wv, wo, out,
-    toks, rows, gb, bb, ws, lg, lg_send, lg_recv, wt_all, wt, back, fill, load_sem, own_sem, send_sem, recv_sem,
+    toks, stage, rows, gb, bb, ws, lg, lg_send, lg_recv, wt_all, wt, back, fill, load_sem, own_sem, send_sem, recv_sem,
 ):
     me = lax.axis_index("col")
     sd, cd, width = toks.shape[1:]
@@ -77,7 +87,10 @@
         loads.append(pltpu.make_async_copy(w, ws.at[k], load_sem.at[k]))
     loads.append(pltpu.make_async_copy(gain, gb, load_sem.at[4]))
     loads.append(pltpu.make_async_copy(bias, bb, load_sem.at[5]))
-    own_in = pltpu.make_async_copy(x.at[pl.ds(me * sd, sd)], toks.at[me], own_sem.at[0])
+    staged = pltpu.make_async_copy(x, stage, own_sem.at[0])
+    staged.start()
+    for k in (0, 1, 4, 5, 2, 3):
+        loads[k].start()
     pl.semaphore_wait(barrier, n - 1)
 
     def remote(src, dst, phase, p):
@@ -86,19 +99,18 @@
             device_id={"col": p}, device_id_type=MESH,
         ).start()
 
+    staged.wait()
+
     def send_tokens(k):
-        p = peer(k + 1)
-        remote(x.at[pl.ds(p * sd, sd)], toks.at[me], 0, p)
-
-    each(n - 1, send_tokens)
-    own_in.start()
-    for k in (4, 5, 0, 1, 2, 3):
-        loads[k].start()
+        p = peer(k)
+        remote(stage.at[pl.ds(p * sd, sd)], toks.at[me], 0, p)
+
+    around(n, send_tokens)
+    toks[me] = stage[pl.ds(me * sd, sd)]
     loads[4].wait()
     loads[5].wait()
     gain_f = gb[...].astype(jnp.float32).reshape(1, width)
     bias_f = bb[...].astype(jnp.float32).reshape(1, width)
-    own_in.wait()
     others = pl.ds(0, n - 1)
     drain(toks.at[others], recv_sem.at[0])
 
@@ -153,10 +165,10 @@
     lg_recv[me] = lg_send[me]
 
     def send_logits(k):
-        p = peer(k + 1)
+        p = peer(k)
         remote(lg_send.at[p], lg_recv.at[me], 1, p)
 
-    each(n - 1, send_logits)
+    around(n, send_logits)
 
     loads[2].wait()
     vals = project(2, 1.0)
@@ -187,9 +199,9 @@
         wt_all[me, :, part] = (expo / norm).astype(jnp.bfloat16)
 
     def send_weights(k):
-        remote(wt_all.at[me], wt_all.at[me], 2, peer(k + 1))
-
-    each(n - 1, send_weights)
+        remote(wt_all.at[me], wt_all.at[me], 2, peer(k))
+
+    around(n, send_weights)
     loads[3].wait()
     drain(wt_all.at[others], recv_sem.at[2])
 
@@ -219,10 +231,10 @@
         scatter_rows(n, cd, fill.at[pl.ds(s * cols, cols)], pack_back)
 
     def send_back(k):
-        p = peer(k + 1)
+        p = peer(k)
         remote(back.at[p], out.at[pl.ds(me * sd, sd)], 3, p)
 
-    each(n - 1, send_back)
+    around(n, send_back)
     own_out = pltpu.make_async_copy(back.at[me], out.at[pl.ds(me * sd, sd)], own_sem.at[1])
     own_out.start()
     drain(toks.at[others], send_sem.at[0])
@@ -242,11 +254,12 @@
     anywhere = pl.BlockSpec(memory_space=pl.ANY)
     return pl.pallas_call(
         functools.partial(kernel, n),
-        out_shape=jax.ShapeDtypeStruct(x.shape, bf),
+        out_shape=pltpu.VMEM(x.shape, bf),
         in_specs=[anywhere] * 7,
-        out_specs=anywhere,
+        out_specs=pl.BlockSpec(memory_space=pltpu.VMEM),
         scratch_shapes=[
             pltpu.VMEM((n, sd, cd, width), bf),
+            pltpu.VMEM(x.shape, bf),
             pltpu.VMEM((tokens, width), f32),
             pltpu.VMEM((width,), bf),
             pltpu.VMEM((width,), bf),

time: 27 us -> 25 us (0.926)
  Pallas kernels: 25.2 us -> 24.2 us
  local copies, waits for them, and re-layouts: 1.6 us -> 0.64 us
    pallas_call x1, Pallas kernels: 25.2 us -> 24.2 us  [local(): pl.pallas_call(functools.partial(kernel, n), out_shape=pltpu.VMEM(x.shape...]
    unnamed x1, local copies, waits for them, and re-layouts: 1.6 us -> 0.64 us
where the time goes in v2:
time: 25 us; the launch traced here: 24.9 us
  Pallas kernels  24.2 us (97%)
  local copies, waits for them, and re-layouts  0.64 us (3%)
    pallas_call x1, Pallas kernels, local(): pl.pallas_call(functools.partial(kernel, n), out_shape=pltpu.VMEM(x.shape...  24.2 us
    unnamed x1, local copies, waits for them, and re-layouts  0.64 us

profile of v2, /device:TPU:0, one launch (start us, length us, event | category | flops | bytes accessed | tf_op | source)
XLA Modules:
  0.0 24.9 jit_solution(96923475181735845)
XLA Ops:
  0.0 24.2 %shard_map.73 = bf16[32,2,768]{2,1,0:T(2,128)(2,1)S(1)} custom-call(bf16[32,2,768]{2,1,0:T(2,128)(2,1)} %x.1, bf16[768]{0:T(1024)(128)(2,1)} %gain.1, bf16[768]{0:T(1024)(128)(2,1)} %bias.1, bf16[768,768]{1,0:T(8,128)(2,1)} %wq.1, bf16[768,768]{1,0:T(8,128)(2,1)} %wk.1, bf16[768,768]{1,0:T(8,128)(2,1)} %wv.1, bf16[768,768]{1,0:T(8,128)(2,1)} %wo.1), custom_call_target="tpu_custom_call" | custom-call | tf_op jit(solution)/shard_map/pallas_call | solution.py:255
  24.2 0.6 %copy.9 = bf16[32,2,768]{2,1,0:T(2,128)(2,1)} copy(bf16[32,2,768]{2,1,0:T(2,128)(2,1)S(1)} %shard_map.73) | data formatting | bytes 196608

commit v3 on v2

--- a/solution.py
+++ b/solution.py
@@ -89,8 +89,23 @@
     loads.append(pltpu.make_async_copy(bias, bb, load_sem.at[5]))
     staged = pltpu.make_async_copy(x, stage, own_sem.at[0])
     staged.start()
-    for k in (0, 1, 4, 5, 2, 3):
+    for k in (4, 5, 0, 1, 2, 3):
         loads[k].start()
+    loads[4].wait()
+    loads[5].wait()
+    gain_f = gb[...].astype(jnp.float32).reshape(1, 1, width)
+    bias_f = bb[...].astype(jnp.float32).reshape(1, 1, width)
+    staged.wait()
+
+    def normalize(p):
+        block = pl.ds(p * sd, sd)
+        a = stage[block].astype(jnp.float32)
+        center = jnp.sum(a, axis=-1, keepdims=True) * (1.0 / width)
+        shifted = a - center
+        spread = jnp.sum(shifted * shifted, axis=-1, keepdims=True) * (1.0 / width)
+        stage[block] = (shifted * lax.rsqrt(spread + 1e-05) * gain_f + bias_f).astype(jnp.bfloat16)
+
+    each(n, normalize)
     pl.semaphore_wait(barrier, n - 1)
 
     def remote(src, dst, phase, p):
@@ -99,18 +114,12 @@
             device_id={"col": p}, device_id_type=MESH,
         ).start()
 
-    staged.wait()
-
     def send_tokens(k):
         p = peer(k)
         remote(stage.at[pl.ds(p * sd, sd)], toks.at[me], 0, p)
 
     around(n, send_tokens)
     toks[me] = stage[pl.ds(me * sd, sd)]
-    loads[4].wait()
-    loads[5].wait()
-    gain_f = gb[...].astype(jnp.float32).reshape(1, width)
-    bias_f = bb[...].astype(jnp.float32).reshape(1, width)
     others = pl.ds(0, n - 1)
     drain(toks.at[others], recv_sem.at[0])
 
@@ -118,11 +127,7 @@
         gather_rows(
             n, cd, lambda p: toks[p, s].astype(jnp.float32), rows.at[pl.ds(s * cols, cols)]
         )
-    a = rows[...]
-    center = jnp.sum(a, axis=-1, keepdims=True) * (1.0 / width)
-    shifted = a - center
-    spread = jnp.sum(shifted * shifted, axis=-1, keepdims=True) * (1.0 / width)
-    normed = (shifted * lax.rsqrt(spread + 1e-05) * gain_f + bias_f).astype(jnp.bfloat16)
+    normed = rows[...].astype(jnp.bfloat16)
 
     def project(k, factor):
         product = jnp.dot(normed, ws[k], preferred_element_type=jnp.float32)

time: 25 us -> 24.8 us (level)
  no operation moved by 1% of the time
where the time goes in v3:
time: 24.8 us; the launch traced here: 24.7 us
  Pallas kernels  24 us (97%)
  local copies, waits for them, and re-layouts  0.64 us (3%)
    pallas_call x1, Pallas kernels, local(): pl.pallas_call(functools.partial(kernel, n), out_shape=pltpu.VMEM(x.shape...  24 us
    unnamed x1, local copies, waits for them, and re-layouts  0.64 us

profile of v3, /device:TPU:0, one launch (start us, length us, event | category | flops | bytes accessed | tf_op | source)
XLA Modules:
  0.0 24.7 jit_solution(10473671012209473894)
XLA Ops:
  0.0 24.0 %shard_map.73 = bf16[32,2,768]{2,1,0:T(2,128)(2,1)S(1)} custom-call(bf16[32,2,768]{2,1,0:T(2,128)(2,1)} %x.1, bf16[768]{0:T(1024)(128)(2,1)} %gain.1, bf16[768]{0:T(1024)(128)(2,1)} %bias.1, bf16[768,768]{1,0:T(8,128)(2,1)} %wq.1, bf16[768,768]{1,0:T(8,128)(2,1)} %wk.1, bf16[768,768]{1,0:T(8,128)(2,1)} %wv.1, bf16[768,768]{1,0:T(8,128)(2,1)} %wo.1), custom_call_target="tpu_custom_call" | custom-call | tf_op jit(solution)/shard_map/pallas_call | solution.py:260
  24.0 0.6 %copy.9 = bf16[32,2,768]{2,1,0:T(2,128)(2,1)} copy(bf16[32,2,768]{2,1,0:T(2,128)(2,1)S(1)} %shard_map.73) | data formatting | bytes 196608
